TPU v7x, 256 devices: a whole 4x4x8 slice. The times are simulated.
256 devices in a mesh: ctx: 32 (over z, y_lo, core), tr: 2 (over y_hi), tc: 4 (over x).
Axes of the slice: x: 4, y: 4 (y_hi: 2, y_lo: 2; y = y_hi * 2 + y_lo), z: 8, core: 2. Of those that a mesh axis runs over, the one named last changes fastest.
Arguments:
- hidden: bfloat16 [16384, 4096], P(('ctx', 'tc'), 'tr'), may hold values from -6 to 6
- norm_gain: float32 [4096], P('tr'), may hold values from 0.25 to 1.75
- seg_lengths: int32 [64], replicated, may hold values from 1 to 512, 16384 in all
- q_weight: bfloat16 [4096, 2048], P('tr', 'tc'), may hold values from -3 to 3
- key_matrix: bfloat16 [4096, 512], P('tr', 'tc'), may hold values from -3 to 3
- value_matrix: bfloat16 [4096, 512], P('tr', 'tc'), may hold values from -0.09375 to 0.09375
- o_weight: bfloat16 [2048, 4096], P('tc', 'tr'), may hold values from -0.125 to 0.125
Outputs:
- layer_out: bfloat16 [16384, 4096], P(('ctx', 'tc'), 'tr')
Inputs may be any that keep to these rules, and one draw needn't show every extreme that they name: `seg_lengths`: entry 0 is the length of the shared prefix, the other entries the candidates' lengths in list order; all sum to 16384, and the longest is exactly 512.
All inputs are finite; a program needn't handle non-finite values.
Results may differ from a plain program's by a relative error of at most 0.01.
Values may be sent and summed in bfloat16 or wider, within the bound.
No kernel may reach another device: no remote copies, remote signals or barrier semaphores. Data moves between devices by JAX's collectives and lax.ppermute only.
A program may use at most 64 MiB of HBM per device.

v0:
```python
import jax
import jax.numpy as jnp
from jax import lax
from jax.sharding import PartitionSpec as P

D = 4096
HEAD_SIZE = 128
epsilon = 1e-05
rope_base = 500000.0
masked_score = -1e30


def from_behind(block, axis, distance):
    devices = range(lax.axis_size(axis))
    route = [(i - distance, i) for i in devices if i - distance in devices]
    return lax.ppermute(block, axis, route)


def rotate(heads_data, positions):
    half_dim = heads_data.shape[-1] // 2
    frequency = rope_base ** (
        -(jnp.arange(half_dim, dtype=jnp.float32) * 2.0 / heads_data.shape[-1])
    )
    angles = positions.astype(jnp.float32)[:, None] * frequency[None, :]
    cosine = jnp.cos(angles)[:, None, :]
    sine_part = jnp.sin(angles)[:, None, :]
    first = heads_data[..., :half_dim]
    second = heads_data[..., half_dim:]
    return jnp.concatenate(
        [first * cosine - second * sine_part, second * cosine + first * sine_part], axis=-1
    )


def segment_of(positions, seg_lengths):
    bounds = jnp.cumsum(seg_lengths)[:-1]
    return jnp.sum((positions[:, None] >= bounds[None, :]).astype(jnp.int32), axis=1)


def per_device(hidden, norm_gain, seg_lengths, q_weight, key_matrix, value_matrix, o_weight):
    wide_hidden = hidden.astype(jnp.float32)
    squares = lax.psum(jnp.sum(wide_hidden * wide_hidden, axis=1), "tr")
    normed_local = (wide_hidden * lax.rsqrt(squares[:, None] / D + epsilon) * norm_gain).astype(
        jnp.bfloat16
    )
    normalized_rows = lax.all_gather(normed_local, "tc", axis=0, tiled=True)
    rows_per_block = normalized_rows.shape[0]
    query_rows = rows_per_block // lax.axis_size("tr")
    query_width = q_weight.shape[1]
    key_width = key_matrix.shape[1]
    summed = lax.psum_scatter(
        jnp.concatenate(
            [
                jnp.dot(normalized_rows, q_weight, preferred_element_type=jnp.float32),
                jnp.dot(normalized_rows, key_matrix, preferred_element_type=jnp.float32),
                jnp.dot(normalized_rows, value_matrix, preferred_element_type=jnp.float32),
            ],
            axis=1,
        ),
        "tr",
        scatter_dimension=0,
        tiled=True,
    )
    cycle_index = lax.axis_index("ctx")
    cycle_size = lax.axis_size("ctx")
    query_pos = (
        cycle_index * rows_per_block
        + lax.axis_index("tr") * query_rows
        + jnp.arange(query_rows, dtype=jnp.int32)
    )
    head_local = query_width // HEAD_SIZE
    key_heads = key_width // HEAD_SIZE
    head_groups = head_local // key_heads
    queries = rotate(summed[:, :query_width].reshape(query_rows, head_local, HEAD_SIZE), query_pos)
    queries = queries.astype(jnp.bfloat16).reshape(query_rows, key_heads, head_groups, HEAD_SIZE)
    key_block_list = rotate(
        summed[:, query_width : query_width + key_width].reshape(query_rows, key_heads, HEAD_SIZE),
        query_pos,
    )
    key_block_list = key_block_list.astype(jnp.bfloat16)
    value_block_list = summed[:, query_width + key_width :].astype(jnp.bfloat16)
    local_pairs = jnp.concatenate(
        [key_block_list.reshape(query_rows, key_width), value_block_list], axis=1
    )
    query_seg = segment_of(query_pos, seg_lengths)
    score_scale = HEAD_SIZE ** (-0.5)

    def attend(softmax_state, key_block, source):
        running_max, weight_sum, accumulated = softmax_state
        key_pos = source * rows_per_block + jnp.arange(rows_per_block, dtype=jnp.int32)
        key_seg = segment_of(key_pos, seg_lengths)
        visible = (key_pos[None, :] <= query_pos[:, None]) & (
            (key_seg[None, :] == 0) | (key_seg[None, :] == query_seg[:, None])
        )
        block_keys = key_block[:, :key_width].reshape(rows_per_block, key_heads, HEAD_SIZE)
        block_values = key_block[:, key_width:].reshape(rows_per_block, key_heads, HEAD_SIZE)
        scores = (
            jnp.einsum("qhgd,khd->hgqk", queries, block_keys, preferred_element_type=jnp.float32)
            * score_scale
        )
        scores = jnp.where(visible, scores, masked_score)
        new_max = jnp.maximum(running_max, jnp.max(scores, axis=-1))
        factor = jnp.exp(running_max - new_max)
        weights = jnp.where(visible, jnp.exp(scores - new_max[..., None]), 0.0)
        weight_sum = weight_sum * factor + jnp.sum(weights, axis=-1)
        accumulated = accumulated * factor[..., None] + jnp.einsum(
            "hgqk,khd->hgqd",
            weights.astype(jnp.bfloat16),
            block_values,
            preferred_element_type=jnp.float32,
        )
        return (new_max, weight_sum, accumulated)

    def maybe_attend(softmax_state, key_block, step_number):
        source = (cycle_index - step_number) % cycle_size
        needed = step_number <= cycle_index
        return lax.cond(
            needed,
            lambda current: attend(current, key_block, source),
            lambda current: current,
            softmax_state,
        )

    state_shape = (key_heads, head_groups, query_rows)
    softmax_state = (
        jnp.full(state_shape, masked_score, jnp.float32),
        jnp.zeros(state_shape, jnp.float32),
        jnp.zeros(state_shape + (HEAD_SIZE,), jnp.float32),
    )
    key_block = lax.all_gather(local_pairs, "tr", axis=0, tiled=True)
    softmax_state = maybe_attend(softmax_state, key_block, 0)

    def advance(step_number, loop_carry):
        moving, current = loop_carry
        moving = from_behind(moving, "ctx", 1)
        return (moving, maybe_attend(current, moving, step_number))

    key_block, softmax_state = lax.fori_loop(1, cycle_size, advance, (key_block, softmax_state))
    running_max, weight_sum, accumulated = softmax_state
    mixed = accumulated / weight_sum[..., None]
    attended = (
        jnp.transpose(mixed, (2, 0, 1, 3)).reshape(query_rows, query_width).astype(jnp.bfloat16)
    )
    partial_terms = jnp.dot(
        lax.all_gather(attended, "tr", axis=0, tiled=True),
        o_weight,
        preferred_element_type=jnp.float32,
    )
    summed_out = lax.psum_scatter(
        partial_terms.astype(jnp.bfloat16), "tc", scatter_dimension=0, tiled=True
    ).astype(jnp.float32)
    return (wide_hidden + summed_out).astype(jnp.bfloat16)


def solution(mesh):
    in_specs = (
        P(("ctx", "tc"), "tr"),
        P("tr"),
        P(),
        P("tr", "tc"),
        P("tr", "tc"),
        P("tr", "tc"),
        P("tc", "tr"),
    )
    out_specs = P(("ctx", "tc"), "tr")
    return jax.shard_map(
        per_device, mesh=mesh, in_specs=in_specs, out_specs=out_specs, check_vma=False
    )
```

profile of v0, /device:TPU:1, one launch (start us, length us, event | category | flops | bytes accessed | tf_op | source)
XLA Modules:
  0.0 513.1 jit_solution(15915280285968883886)
XLA Ops:
  7.9 6.0 %psum.7 = f32[128]{0:T(128)S(1)} all-reduce(f32[128]{0:T(128)S(1)} %fusion.40), channel_id=1, replica_groups=mesh['ctx'=32,'tr'=2,'tc'=4] {'tr'}, use_global_device_ids=true, to_apply=%region_1.0 | all-reduce | flops 128 | bytes 1024 | tf_op jit(solution)/shard_map/psum | solution.py:41
  16.1 37.7 %all-gather.2.cloned.1.call-done = bf16[512,2048]{1,0:T(8,128)(2,1)} async-done(((bf16[128,2048]{1,0:T(8,128)(2,1)}), bf16[512,2048]{1,0:T(8,128)(2,1)}) %all-gather.2.cloned.1.call-update) | async-done | bytes 2097168 | tf_op jit(solution)/shard_map/all_gather | solution.py:45
  62.3 31.2 %reduce-scatter.3.cloned.1.call-done = f32[256,768]{0,1:T(8,128)} async-done(((f32[512,768]{0,1:T(8,128)}), f32[256,768]{0,1:T(8,128)}) %reduce-scatter.3.cloned.1.call-update) | async-done | bytes 786448 | tf_op jit(solution)/shard_map/reduce_scatter | solution.py:50
  100.3 6.5 %all_gather.10 = bf16[512,256]{0,1:T(8,128)(2,1)S(1)} all-gather(bf16[256,256]{0,1:T(8,128)(2,1)S(1)} %pad_maximum_fusion.2), channel_id=1, replica_groups=mesh['ctx'=32,'tr'=2,'tc'=4] {'tr'}, dimensions={0}, use_global_device_ids=true | all-gather | bytes 393216 | tf_op jit(solution)/shard_map/all_gather | solution.py:129
  113.1 279.2 %while.22 = (s32[]{:T(128)}, bf16[512,256]{1,0:T(8,128)(2,1)S(1)}, f32[1,4,256]{2,1,0:T(4,128)S(1)}, f32[1,4,256]{2,1,0:T(4,128)S(1)}, f32[1,4,256,128]{3,2,1,0:...) while((s32[]{:T(128)}, bf16[512,256]{1,0:T(8,128)(2,1)S(1)}, ...), condition=%wide.region_18.19_spmd.clone, body=%wide.region_11.18_spmd.clone.sunk | while | flops 276142272 | bytes 10047672 | solution.py:137
  130.5 7.1 %collective-permute-start = (bf16[512,256]{1,0:T(8,128)(2,1)S(1)}, bf16[512,256]{1,0:T(8,128)(2,1)S(1)}, u32[]{:S(2)}, u32[]{:S(2)}) collective-permute-start(bf16[512,256]{1,0:T(8,128)(2,1)S(1)} %get-tuple-element.707), channel_id=1, source_target_pairs={{0,8},{8,16},{16,24},{24,32},{32,40},{40,48},{48,56},{56,64},{64,7... | collective-permute-start | bytes 786440 | tf_op jit(solution)/shard_map/while/body/eval_jaxpr/ppermute | solution.py:16
  164.9 8.0 %collective-permute-start = (bf16[512,256]{1,0:T(8,128)(2,1)S(1)}, bf16[512,256]{1,0:T(8,128)(2,1)S(1)}, u32[]{:S(2)}, u32[]{:S(2)}) collective-permute-start(bf16[512,256]{1,0:T(8,128)(2,1)S(1)} %get-tuple-element.707), channel_id=1, source_target_pairs={{0,8},{8,16},{16,24},{24,32},{32,40},{40,48},{48,56},{56,64},{64,7... | collective-permute-start | bytes 786440 | tf_op jit(solution)/shard_map/while/body/eval_jaxpr/ppermute | solution.py:16
  176.2 5.3 %collective-permute-start = (bf16[512,256]{1,0:T(8,128)(2,1)S(1)}, bf16[512,256]{1,0:T(8,128)(2,1)S(1)}, u32[]{:S(2)}, u32[]{:S(2)}) collective-permute-start(bf16[512,256]{1,0:T(8,128)(2,1)S(1)} %get-tuple-element.707), channel_id=1, source_target_pairs={{0,8},{8,16},{16,24},{24,32},{32,40},{40,48},{48,56},{56,64},{64,7... | collective-permute-start | bytes 786440 | tf_op jit(solution)/shard_map/while/body/eval_jaxpr/ppermute | solution.py:16
  193.4 5.3 %collective-permute-start = (bf16[512,256]{1,0:T(8,128)(2,1)S(1)}, bf16[512,256]{1,0:T(8,128)(2,1)S(1)}, u32[]{:S(2)}, u32[]{:S(2)}) collective-permute-start(bf16[512,256]{1,0:T(8,128)(2,1)S(1)} %get-tuple-element.707), channel_id=1, source_target_pairs={{0,8},{8,16},{16,24},{24,32},{32,40},{40,48},{48,56},{56,64},{64,7... | collective-permute-start | bytes 786440 | tf_op jit(solution)/shard_map/while/body/eval_jaxpr/ppermute | solution.py:16
  202.1 5.3 %collective-permute-start = (bf16[512,256]{1,0:T(8,128)(2,1)S(1)}, bf16[512,256]{1,0:T(8,128)(2,1)S(1)}, u32[]{:S(2)}, u32[]{:S(2)}) collective-permute-start(bf16[512,256]{1,0:T(8,128)(2,1)S(1)} %get-tuple-element.707), channel_id=1, source_target_pairs={{0,8},{8,16},{16,24},{24,32},{32,40},{40,48},{48,56},{56,64},{64,7... | collective-permute-start | bytes 786440 | tf_op jit(solution)/shard_map/while/body/eval_jaxpr/ppermute | solution.py:16
  219.3 5.3 %collective-permute-start = (bf16[512,256]{1,0:T(8,128)(2,1)S(1)}, bf16[512,256]{1,0:T(8,128)(2,1)S(1)}, u32[]{:S(2)}, u32[]{:S(2)}) collective-permute-start(bf16[512,256]{1,0:T(8,128)(2,1)S(1)} %get-tuple-element.707), channel_id=1, source_target_pairs={{0,8},{8,16},{16,24},{24,32},{32,40},{40,48},{48,56},{56,64},{64,7... | collective-permute-start | bytes 786440 | tf_op jit(solution)/shard_map/while/body/eval_jaxpr/ppermute | solution.py:16
  228.0 5.3 %collective-permute-start = (bf16[512,256]{1,0:T(8,128)(2,1)S(1)}, bf16[512,256]{1,0:T(8,128)(2,1)S(1)}, u32[]{:S(2)}, u32[]{:S(2)}) collective-permute-start(bf16[512,256]{1,0:T(8,128)(2,1)S(1)} %get-tuple-element.707), channel_id=1, source_target_pairs={{0,8},{8,16},{16,24},{24,32},{32,40},{40,48},{48,56},{56,64},{64,7... | collective-permute-start | bytes 786440 | tf_op jit(solution)/shard_map/while/body/eval_jaxpr/ppermute | solution.py:16
  236.6 5.3 %collective-permute-start = (bf16[512,256]{1,0:T(8,128)(2,1)S(1)}, bf16[512,256]{1,0:T(8,128)(2,1)S(1)}, u32[]{:S(2)}, u32[]{:S(2)}) collective-permute-start(bf16[512,256]{1,0:T(8,128)(2,1)S(1)} %get-tuple-element.707), channel_id=1, source_target_pairs={{0,8},{8,16},{16,24},{24,32},{32,40},{40,48},{48,56},{56,64},{64,7... | collective-permute-start | bytes 786440 | tf_op jit(solution)/shard_map/while/body/eval_jaxpr/ppermute | solution.py:16
  245.2 5.3 %collective-permute-start = (bf16[512,256]{1,0:T(8,128)(2,1)S(1)}, bf16[512,256]{1,0:T(8,128)(2,1)S(1)}, u32[]{:S(2)}, u32[]{:S(2)}) collective-permute-start(bf16[512,256]{1,0:T(8,128)(2,1)S(1)} %get-tuple-element.707), channel_id=1, source_target_pairs={{0,8},{8,16},{16,24},{24,32},{32,40},{40,48},{48,56},{56,64},{64,7... | collective-permute-start | bytes 786440 | tf_op jit(solution)/shard_map/while/body/eval_jaxpr/ppermute | solution.py:16
  262.5 5.3 %collective-permute-start = (bf16[512,256]{1,0:T(8,128)(2,1)S(1)}, bf16[512,256]{1,0:T(8,128)(2,1)S(1)}, u32[]{:S(2)}, u32[]{:S(2)}) collective-permute-start(bf16[512,256]{1,0:T(8,128)(2,1)S(1)} %get-tuple-element.707), channel_id=1, source_target_pairs={{0,8},{8,16},{16,24},{24,32},{32,40},{40,48},{48,56},{56,64},{64,7... | collective-permute-start | bytes 786440 | tf_op jit(solution)/shard_map/while/body/eval_jaxpr/ppermute | solution.py:16
  271.1 5.3 %collective-permute-start = (bf16[512,256]{1,0:T(8,128)(2,1)S(1)}, bf16[512,256]{1,0:T(8,128)(2,1)S(1)}, u32[]{:S(2)}, u32[]{:S(2)}) collective-permute-start(bf16[512,256]{1,0:T(8,128)(2,1)S(1)} %get-tuple-element.707), channel_id=1, source_target_pairs={{0,8},{8,16},{16,24},{24,32},{32,40},{40,48},{48,56},{56,64},{64,7... | collective-permute-start | bytes 786440 | tf_op jit(solution)/shard_map/while/body/eval_jaxpr/ppermute | solution.py:16
  288.4 5.3 %collective-permute-start = (bf16[512,256]{1,0:T(8,128)(2,1)S(1)}, bf16[512,256]{1,0:T(8,128)(2,1)S(1)}, u32[]{:S(2)}, u32[]{:S(2)}) collective-permute-start(bf16[512,256]{1,0:T(8,128)(2,1)S(1)} %get-tuple-element.707), channel_id=1, source_target_pairs={{0,8},{8,16},{16,24},{24,32},{32,40},{40,48},{48,56},{56,64},{64,7... | collective-permute-start | bytes 786440 | tf_op jit(solution)/shard_map/while/body/eval_jaxpr/ppermute | solution.py:16
  297.0 5.3 %collective-permute-start = (bf16[512,256]{1,0:T(8,128)(2,1)S(1)}, bf16[512,256]{1,0:T(8,128)(2,1)S(1)}, u32[]{:S(2)}, u32[]{:S(2)}) collective-permute-start(bf16[512,256]{1,0:T(8,128)(2,1)S(1)} %get-tuple-element.707), channel_id=1, source_target_pairs={{0,8},{8,16},{16,24},{24,32},{32,40},{40,48},{48,56},{56,64},{64,7... | collective-permute-start | bytes 786440 | tf_op jit(solution)/shard_map/while/body/eval_jaxpr/ppermute | solution.py:16
  314.3 5.3 %collective-permute-start = (bf16[512,256]{1,0:T(8,128)(2,1)S(1)}, bf16[512,256]{1,0:T(8,128)(2,1)S(1)}, u32[]{:S(2)}, u32[]{:S(2)}) collective-permute-start(bf16[512,256]{1,0:T(8,128)(2,1)S(1)} %get-tuple-element.707), channel_id=1, source_target_pairs={{0,8},{8,16},{16,24},{24,32},{32,40},{40,48},{48,56},{56,64},{64,7... | collective-permute-start | bytes 786440 | tf_op jit(solution)/shard_map/while/body/eval_jaxpr/ppermute | solution.py:16
  357.4 9.1 %collective-permute-start = (bf16[512,256]{1,0:T(8,128)(2,1)S(1)}, bf16[512,256]{1,0:T(8,128)(2,1)S(1)}, u32[]{:S(2)}, u32[]{:S(2)}) collective-permute-start(bf16[512,256]{1,0:T(8,128)(2,1)S(1)} %get-tuple-element.707), channel_id=1, source_target_pairs={{0,8},{8,16},{16,24},{24,32},{32,40},{40,48},{48,56},{56,64},{64,7... | collective-permute-start | bytes 786440 | tf_op jit(solution)/shard_map/while/body/eval_jaxpr/ppermute | solution.py:16
  369.9 6.5 %collective-permute-start = (bf16[512,256]{1,0:T(8,128)(2,1)S(1)}, bf16[512,256]{1,0:T(8,128)(2,1)S(1)}, u32[]{:S(2)}, u32[]{:S(2)}) collective-permute-start(bf16[512,256]{1,0:T(8,128)(2,1)S(1)} %get-tuple-element.707), channel_id=1, source_target_pairs={{0,8},{8,16},{16,24},{24,32},{32,40},{40,48},{48,56},{56,64},{64,7... | collective-permute-start | bytes 786440 | tf_op jit(solution)/shard_map/while/body/eval_jaxpr/ppermute | solution.py:16
  379.7 9.2 %collective-permute-start = (bf16[512,256]{1,0:T(8,128)(2,1)S(1)}, bf16[512,256]{1,0:T(8,128)(2,1)S(1)}, u32[]{:S(2)}, u32[]{:S(2)}) collective-permute-start(bf16[512,256]{1,0:T(8,128)(2,1)S(1)} %get-tuple-element.707), channel_id=1, source_target_pairs={{0,8},{8,16},{16,24},{24,32},{32,40},{40,48},{48,56},{56,64},{64,7... | collective-permute-start | bytes 786440 | tf_op jit(solution)/shard_map/while/body/eval_jaxpr/ppermute | solution.py:16
  392.5 7.4 %all_gather.11 = bf16[512,512]{0,1:T(8,128)(2,1)S(1)} all-gather(bf16[256,512]{0,1:T(8,128)(2,1)S(1)} %bitcast.110), channel_id=1, replica_groups=mesh['ctx'=32,'tr'=2,'tc'=4] {'tr'}, dimensions={0}, use_global_device_ids=true | all-gather | bytes 786432 | tf_op jit(solution)/shard_map/all_gather | solution.py:144
  402.5 102.1 %reduce-scatter.5.cloned.1.call-done = bf16[128,2048]{1,0:T(8,128)(2,1)} async-done(((bf16[512,2048]{1,0:T(8,128)(2,1)}), bf16[128,2048]{1,0:T(8,128)(2,1)}) %reduce-scatter.5.cloned.1.call-update) | async-done | bytes 524304 | tf_op jit(solution)/shard_map/reduce_scatter | solution.py:148
  (220 shorter events, 211.0 us)
Async XLA Ops:
  6.5 47.2 %all-gather.2.cloned.1.call-start = ((), (), s32[]{:S(2)}) async-start(), calls=%async_computation.2 | async-start | bytes 2621440 | tf_op jit(solution)/shard_map/all_gather | solution.py:45
  16.0 77.5 %reduce-scatter.3.cloned.1.call-start = ((), (), s32[]{:S(2)}) async-start(), calls=%async_computation.3 | async-start | bytes 2359296 | tf_op jit(solution)/shard_map/reduce_scatter | solution.py:50
  60.6 444.0 %reduce-scatter.5.cloned.1.call-start = ((), (), s32[]{:S(2)}) async-start(), calls=%async_computation.4 | async-start | bytes 2621440 | tf_op jit(solution)/shard_map/reduce_scatter | solution.py:148
  130.5 10.4 %collective-permute-start = (bf16[512,256]{1,0:T(8,128)(2,1)S(1)}, bf16[512,256]{1,0:T(8,128)(2,1)S(1)}, u32[]{:S(2)}, u32[]{:S(2)}) collective-permute-start(bf16[512,256]{1,0:T(8,128)(2,1)S(1)} %get-tuple-element.707), channel_id=1, source_target_pairs={{0,8},{8,16},{16,24},{24,32},{32,40},{40,48},{48,56},{56,64},{64,7... | collective-permute-start | bytes 786440 | tf_op jit(solution)/shard_map/while/body/eval_jaxpr/ppermute | solution.py:16
  164.9 11.3 %collective-permute-start = (bf16[512,256]{1,0:T(8,128)(2,1)S(1)}, bf16[512,256]{1,0:T(8,128)(2,1)S(1)}, u32[]{:S(2)}, u32[]{:S(2)}) collective-permute-start(bf16[512,256]{1,0:T(8,128)(2,1)S(1)} %get-tuple-element.707), channel_id=1, source_target_pairs={{0,8},{8,16},{16,24},{24,32},{32,40},{40,48},{48,56},{56,64},{64,7... | collective-permute-start | bytes 786440 | tf_op jit(solution)/shard_map/while/body/eval_jaxpr/ppermute | solution.py:16
  176.2 8.6 %collective-permute-start = (bf16[512,256]{1,0:T(8,128)(2,1)S(1)}, bf16[512,256]{1,0:T(8,128)(2,1)S(1)}, u32[]{:S(2)}, u32[]{:S(2)}) collective-permute-start(bf16[512,256]{1,0:T(8,128)(2,1)S(1)} %get-tuple-element.707), channel_id=1, source_target_pairs={{0,8},{8,16},{16,24},{24,32},{32,40},{40,48},{48,56},{56,64},{64,7... | collective-permute-start | bytes 786440 | tf_op jit(solution)/shard_map/while/body/eval_jaxpr/ppermute | solution.py:16
  184.8 8.6 %collective-permute-start = (bf16[512,256]{1,0:T(8,128)(2,1)S(1)}, bf16[512,256]{1,0:T(8,128)(2,1)S(1)}, u32[]{:S(2)}, u32[]{:S(2)}) collective-permute-start(bf16[512,256]{1,0:T(8,128)(2,1)S(1)} %get-tuple-element.707), channel_id=1, source_target_pairs={{0,8},{8,16},{16,24},{24,32},{32,40},{40,48},{48,56},{56,64},{64,7... | collective-permute-start | bytes 786440 | tf_op jit(solution)/shard_map/while/body/eval_jaxpr/ppermute | solution.py:16
  193.4 8.6 %collective-permute-start = (bf16[512,256]{1,0:T(8,128)(2,1)S(1)}, bf16[512,256]{1,0:T(8,128)(2,1)S(1)}, u32[]{:S(2)}, u32[]{:S(2)}) collective-permute-start(bf16[512,256]{1,0:T(8,128)(2,1)S(1)} %get-tuple-element.707), channel_id=1, source_target_pairs={{0,8},{8,16},{16,24},{24,32},{32,40},{40,48},{48,56},{56,64},{64,7... | collective-permute-start | bytes 786440 | tf_op jit(solution)/shard_map/while/body/eval_jaxpr/ppermute | solution.py:16
  202.1 8.6 %collective-permute-start = (bf16[512,256]{1,0:T(8,128)(2,1)S(1)}, bf16[512,256]{1,0:T(8,128)(2,1)S(1)}, u32[]{:S(2)}, u32[]{:S(2)}) collective-permute-start(bf16[512,256]{1,0:T(8,128)(2,1)S(1)} %get-tuple-element.707), channel_id=1, source_target_pairs={{0,8},{8,16},{16,24},{24,32},{32,40},{40,48},{48,56},{56,64},{64,7... | collective-permute-start | bytes 786440 | tf_op jit(solution)/shard_map/while/body/eval_jaxpr/ppermute | solution.py:16
  210.7 8.6 %collective-permute-start = (bf16[512,256]{1,0:T(8,128)(2,1)S(1)}, bf16[512,256]{1,0:T(8,128)(2,1)S(1)}, u32[]{:S(2)}, u32[]{:S(2)}) collective-permute-start(bf16[512,256]{1,0:T(8,128)(2,1)S(1)} %get-tuple-element.707), channel_id=1, source_target_pairs={{0,8},{8,16},{16,24},{24,32},{32,40},{40,48},{48,56},{56,64},{64,7... | collective-permute-start | bytes 786440 | tf_op jit(solution)/shard_map/while/body/eval_jaxpr/ppermute | solution.py:16
  219.3 8.6 %collective-permute-start = (bf16[512,256]{1,0:T(8,128)(2,1)S(1)}, bf16[512,256]{1,0:T(8,128)(2,1)S(1)}, u32[]{:S(2)}, u32[]{:S(2)}) collective-permute-start(bf16[512,256]{1,0:T(8,128)(2,1)S(1)} %get-tuple-element.707), channel_id=1, source_target_pairs={{0,8},{8,16},{16,24},{24,32},{32,40},{40,48},{48,56},{56,64},{64,7... | collective-permute-start | bytes 786440 | tf_op jit(solution)/shard_map/while/body/eval_jaxpr/ppermute | solution.py:16
  228.0 8.6 %collective-permute-start = (bf16[512,256]{1,0:T(8,128)(2,1)S(1)}, bf16[512,256]{1,0:T(8,128)(2,1)S(1)}, u32[]{:S(2)}, u32[]{:S(2)}) collective-permute-start(bf16[512,256]{1,0:T(8,128)(2,1)S(1)} %get-tuple-element.707), channel_id=1, source_target_pairs={{0,8},{8,16},{16,24},{24,32},{32,40},{40,48},{48,56},{56,64},{64,7... | collective-permute-start | bytes 786440 | tf_op jit(solution)/shard_map/while/body/eval_jaxpr/ppermute | solution.py:16
  236.6 8.6 %collective-permute-start = (bf16[512,256]{1,0:T(8,128)(2,1)S(1)}, bf16[512,256]{1,0:T(8,128)(2,1)S(1)}, u32[]{:S(2)}, u32[]{:S(2)}) collective-permute-start(bf16[512,256]{1,0:T(8,128)(2,1)S(1)} %get-tuple-element.707), channel_id=1, source_target_pairs={{0,8},{8,16},{16,24},{24,32},{32,40},{40,48},{48,56},{56,64},{64,7... | collective-permute-start | bytes 786440 | tf_op jit(solution)/shard_map/while/body/eval_jaxpr/ppermute | solution.py:16
  245.2 8.6 %collective-permute-start = (bf16[512,256]{1,0:T(8,128)(2,1)S(1)}, bf16[512,256]{1,0:T(8,128)(2,1)S(1)}, u32[]{:S(2)}, u32[]{:S(2)}) collective-permute-start(bf16[512,256]{1,0:T(8,128)(2,1)S(1)} %get-tuple-element.707), channel_id=1, source_target_pairs={{0,8},{8,16},{16,24},{24,32},{32,40},{40,48},{48,56},{56,64},{64,7... | collective-permute-start | bytes 786440 | tf_op jit(solution)/shard_map/while/body/eval_jaxpr/ppermute | solution.py:16
  253.8 8.6 %collective-permute-start = (bf16[512,256]{1,0:T(8,128)(2,1)S(1)}, bf16[512,256]{1,0:T(8,128)(2,1)S(1)}, u32[]{:S(2)}, u32[]{:S(2)}) collective-permute-start(bf16[512,256]{1,0:T(8,128)(2,1)S(1)} %get-tuple-element.707), channel_id=1, source_target_pairs={{0,8},{8,16},{16,24},{24,32},{32,40},{40,48},{48,56},{56,64},{64,7... | collective-permute-start | bytes 786440 | tf_op jit(solution)/shard_map/while/body/eval_jaxpr/ppermute | solution.py:16
  262.5 8.6 %collective-permute-start = (bf16[512,256]{1,0:T(8,128)(2,1)S(1)}, bf16[512,256]{1,0:T(8,128)(2,1)S(1)}, u32[]{:S(2)}, u32[]{:S(2)}) collective-permute-start(bf16[512,256]{1,0:T(8,128)(2,1)S(1)} %get-tuple-element.707), channel_id=1, source_target_pairs={{0,8},{8,16},{16,24},{24,32},{32,40},{40,48},{48,56},{56,64},{64,7... | collective-permute-start | bytes 786440 | tf_op jit(solution)/shard_map/while/body/eval_jaxpr/ppermute | solution.py:16
  271.1 8.6 %collective-permute-start = (bf16[512,256]{1,0:T(8,128)(2,1)S(1)}, bf16[512,256]{1,0:T(8,128)(2,1)S(1)}, u32[]{:S(2)}, u32[]{:S(2)}) collective-permute-start(bf16[512,256]{1,0:T(8,128)(2,1)S(1)} %get-tuple-element.707), channel_id=1, source_target_pairs={{0,8},{8,16},{16,24},{24,32},{32,40},{40,48},{48,56},{56,64},{64,7... | collective-permute-start | bytes 786440 | tf_op jit(solution)/shard_map/while/body/eval_jaxpr/ppermute | solution.py:16
  279.7 8.6 %collective-permute-start = (bf16[512,256]{1,0:T(8,128)(2,1)S(1)}, bf16[512,256]{1,0:T(8,128)(2,1)S(1)}, u32[]{:S(2)}, u32[]{:S(2)}) collective-permute-start(bf16[512,256]{1,0:T(8,128)(2,1)S(1)} %get-tuple-element.707), channel_id=1, source_target_pairs={{0,8},{8,16},{16,24},{24,32},{32,40},{40,48},{48,56},{56,64},{64,7... | collective-permute-start | bytes 786440 | tf_op jit(solution)/shard_map/while/body/eval_jaxpr/ppermute | solution.py:16
  288.4 8.6 %collective-permute-start = (bf16[512,256]{1,0:T(8,128)(2,1)S(1)}, bf16[512,256]{1,0:T(8,128)(2,1)S(1)}, u32[]{:S(2)}, u32[]{:S(2)}) collective-permute-start(bf16[512,256]{1,0:T(8,128)(2,1)S(1)} %get-tuple-element.707), channel_id=1, source_target_pairs={{0,8},{8,16},{16,24},{24,32},{32,40},{40,48},{48,56},{56,64},{64,7... | collective-permute-start | bytes 786440 | tf_op jit(solution)/shard_map/while/body/eval_jaxpr/ppermute | solution.py:16
  297.0 8.6 %collective-permute-start = (bf16[512,256]{1,0:T(8,128)(2,1)S(1)}, bf16[512,256]{1,0:T(8,128)(2,1)S(1)}, u32[]{:S(2)}, u32[]{:S(2)}) collective-permute-start(bf16[512,256]{1,0:T(8,128)(2,1)S(1)} %get-tuple-element.707), channel_id=1, source_target_pairs={{0,8},{8,16},{16,24},{24,32},{32,40},{40,48},{48,56},{56,64},{64,7... | collective-permute-start | bytes 786440 | tf_op jit(solution)/shard_map/while/body/eval_jaxpr/ppermute | solution.py:16
  331.5 8.6 %collective-permute-start = (bf16[512,256]{1,0:T(8,128)(2,1)S(1)}, bf16[512,256]{1,0:T(8,128)(2,1)S(1)}, u32[]{:S(2)}, u32[]{:S(2)}) collective-permute-start(bf16[512,256]{1,0:T(8,128)(2,1)S(1)} %get-tuple-element.707), channel_id=1, source_target_pairs={{0,8},{8,16},{16,24},{24,32},{32,40},{40,48},{48,56},{56,64},{64,7... | collective-permute-start | bytes 786440 | tf_op jit(solution)/shard_map/while/body/eval_jaxpr/ppermute | solution.py:16
  357.4 12.4 %collective-permute-start = (bf16[512,256]{1,0:T(8,128)(2,1)S(1)}, bf16[512,256]{1,0:T(8,128)(2,1)S(1)}, u32[]{:S(2)}, u32[]{:S(2)}) collective-permute-start(bf16[512,256]{1,0:T(8,128)(2,1)S(1)} %get-tuple-element.707), channel_id=1, source_target_pairs={{0,8},{8,16},{16,24},{24,32},{32,40},{40,48},{48,56},{56,64},{64,7... | collective-permute-start | bytes 786440 | tf_op jit(solution)/shard_map/while/body/eval_jaxpr/ppermute | solution.py:16
  369.9 9.8 %collective-permute-start = (bf16[512,256]{1,0:T(8,128)(2,1)S(1)}, bf16[512,256]{1,0:T(8,128)(2,1)S(1)}, u32[]{:S(2)}, u32[]{:S(2)}) collective-permute-start(bf16[512,256]{1,0:T(8,128)(2,1)S(1)} %get-tuple-element.707), channel_id=1, source_target_pairs={{0,8},{8,16},{16,24},{24,32},{32,40},{40,48},{48,56},{56,64},{64,7... | collective-permute-start | bytes 786440 | tf_op jit(solution)/shard_map/while/body/eval_jaxpr/ppermute | solution.py:16
  379.7 12.5 %collective-permute-start = (bf16[512,256]{1,0:T(8,128)(2,1)S(1)}, bf16[512,256]{1,0:T(8,128)(2,1)S(1)}, u32[]{:S(2)}, u32[]{:S(2)}) collective-permute-start(bf16[512,256]{1,0:T(8,128)(2,1)S(1)} %get-tuple-element.707), channel_id=1, source_target_pairs={{0,8},{8,16},{16,24},{24,32},{32,40},{40,48},{48,56},{56,64},{64,7... | collective-permute-start | bytes 786440 | tf_op jit(solution)/shard_map/while/body/eval_jaxpr/ppermute | solution.py:16
  (19 other events, 662.7 us)
Sparse Core Ops, SparseCore 0:
  16.1 37.5 all-gather.1
  60.8 32.7 reduce-scatter.2
  402.6 101.9 reduce-scatter.4
where the time goes:
time: 514 us; the launch traced here: 513 us
  waiting for transfers between devices  273 us (53%)
  starting transfers between devices  173 us (34%)
  blocking collectives  20 us (4%)
  between operations  13.3 us (3%)
  other arithmetic  13.2 us (3%)
  matrix products  10.6 us (2%)
  local copies, waits for them, and re-layouts  8.94 us (2%)
    ppermute x31, starting transfers between devices, from_behind(): return lax.ppermute(block, axis, route)  173 us
    reduce_scatter x1, waiting for transfers between devices, per_device(): lax.psum_scatter(partial_terms.astype(jnp.bfloat16), 'tc', scatter_dimens...  102 us
    ppermute x31, waiting for transfers between devices, from_behind(): return lax.ppermute(block, axis, route)  102 us
    all_gather x1, waiting for transfers between devices, per_device(): normalized_rows = lax.all_gather(normed_local, 'tc', axis=0, tiled=True)  37.7 us
    reduce_scatter x1, waiting for transfers between devices, per_device(): lax.psum_scatter(jnp.concatenate([jnp.dot(normalized_rows, q_weight, pref...  31.2 us
  transfers between devices with their start and end apart: 34, of which 34 were waited for; matrix products, arithmetic and copies ran while one was open for 0% of the time, Pallas kernels for 0%

commit v1 on v0

--- a/solution.py
+++ b/solution.py
@@ -8,6 +8,27 @@
 epsilon = 1e-05
 rope_base = 500000.0
 masked_score = -1e30
+
+
+def collect(value, axis, dim):
+    devices, index, width = (lax.axis_size(axis), lax.axis_index(axis), value.shape[dim])
+    forward = [(i, (i + 1) % devices) for i in range(devices)]
+    left = [(i, (i - 1) % devices) for i in range(devices)]
+    whole = jnp.zeros((*value.shape[:dim], devices * width, *value.shape[dim + 1 :]), value.dtype)
+    whole = lax.dynamic_update_slice_in_dim(whole, value, index * width, axis=dim)
+    from_left = from_right = value
+    half = devices // 2
+    for lap in range(1, half + 1):
+        from_left = lax.ppermute(from_left, axis, forward)
+        whole = lax.dynamic_update_slice_in_dim(
+            whole, from_left, (index - lap) % devices * width, axis=dim
+        )
+        if lap < devices - half:
+            from_right = lax.ppermute(from_right, axis, left)
+            whole = lax.dynamic_update_slice_in_dim(
+                whole, from_right, (index + lap) % devices * width, axis=dim
+            )
+    return whole
 
 
 def from_behind(block, axis, distance):
@@ -42,7 +63,7 @@
     normed_local = (wide_hidden * lax.rsqrt(squares[:, None] / D + epsilon) * norm_gain).astype(
         jnp.bfloat16
     )
-    normalized_rows = lax.all_gather(normed_local, "tc", axis=0, tiled=True)
+    normalized_rows = collect(normed_local, "tc", 0)
     rows_per_block = normalized_rows.shape[0]
     query_rows = rows_per_block // lax.axis_size("tr")
     query_width = q_weight.shape[1]

time: 514 us -> 583 us (1.13)
  starting transfers between devices: 173 us -> 201 us
  local copies, waits for them, and re-layouts: 8.94 us -> 35.8 us
  waiting for transfers between devices: 273 us -> 283 us
    all_gather x1 -> x0, waiting for transfers between devices: 37.7 us -> none  [per_device(): normalized_rows = lax.all_gather(normed_local, 'tc', axis=0, tiled=True)]
    ppermute x31, starting transfers between devices: 173 us -> 196 us  [from_behind(): return lax.ppermute(block, axis, route)]
    while x31, local copies, waits for them, and re-layouts: 0.56 us -> 21.8 us
    reduce_scatter x1, waiting for transfers between devices: 102 us -> 118 us  [per_device(): lax.psum_scatter(partial_terms.astype(jnp.bfloat16), 'tc', scatter_dimens...]
    ppermute x0 -> x3, waiting for transfers between devices: none -> 15.4 us  [the longest x2 15.4 us: collect(): from_left = lax.ppermute(from_left, axis, forward)]
    ppermute x31, waiting for transfers between devices: 102 us -> 112 us  [from_behind(): return lax.ppermute(block, axis, route)]
    reduce_scatter x1, waiting for transfers between devices: 31.2 us -> 37.9 us  [per_device(): lax.psum_scatter(jnp.concatenate([jnp.dot(normalized_rows, q_weight, pref...]
  transfers between devices with their start and end apart: 34 -> 36, of which waited for: 34 -> 35; matrix products, arithmetic and copies ran while one was open for 0% -> 1% of each run, Pallas kernels for 0% -> 0%
where the time goes in v1:
time: 583 us; the launch traced here: 580 us
  waiting for transfers between devices  283 us (49%)
  starting transfers between devices  201 us (34%)
  local copies, waits for them, and re-layouts  35.8 us (6%)
  blocking collectives  20.2 us (3%)
  matrix products  15.7 us (3%)
  between operations  13.6 us (2%)
  other arithmetic  10.5 us (2%)
    ppermute x31, starting transfers between devices, from_behind(): return lax.ppermute(block, axis, route)  196 us
    reduce_scatter x1, waiting for transfers between devices, per_device(): lax.psum_scatter(partial_terms.astype(jnp.bfloat16), 'tc', scatter_dimens...  118 us
    ppermute x31, waiting for transfers between devices, from_behind(): return lax.ppermute(block, axis, route)  112 us
    reduce_scatter x1, waiting for transfers between devices, per_device(): lax.psum_scatter(jnp.concatenate([jnp.dot(normalized_rows, q_weight, pref...  37.9 us
    while x31, local copies, waits for them, and re-layouts  21.8 us
    ppermute x2, waiting for transfers between devices, collect(): from_left = lax.ppermute(from_left, axis, forward)  15.4 us
  transfers between devices with their start and end apart: 36, of which 35 were waited for; matrix products, arithmetic and copies ran while one was open for 1% of the time, Pallas kernels for 0%

profile of v1, /device:TPU:1, one launch (start us, length us, event | category | flops | bytes accessed | tf_op | source)
XLA Modules:
  0.0 579.9 jit_solution(14256449168230140061)
XLA Ops:
  7.9 6.0 %psum.7 = f32[128]{0:T(128)S(1)} all-reduce(f32[128]{0:T(128)S(1)} %fusion.40), channel_id=1, replica_groups=mesh['ctx'=32,'tr'=2,'tc'=4] {'tr'}, use_global_device_ids=true, to_apply=%region_1.0 | all-reduce | flops 128 | bytes 1024 | tf_op jit(solution)/shard_map/psum | solution.py:62
  19.4 8.5 %collective-permute-done.1 = bf16[128,2048]{1,0:T(8,128)(2,1)S(1)} collective-permute-done((bf16[128,2048]{1,0:T(8,128)(2,1)}, bf16[128,2048]{1,0:T(8,128)(2,1)S(1)}, u32[]{:S(2)}, u32[]{:S(2)}) %collective-permute-start.1) | collective-permute-done | bytes 524320 | tf_op jit(solution)/shard_map/ppermute | solution.py:22
  32.5 6.8 %collective-permute-done.3 = bf16[128,2048]{1,0:T(8,128)(2,1)} collective-permute-done((bf16[128,2048]{1,0:T(8,128)(2,1)S(1)}, bf16[128,2048]{1,0:T(8,128)(2,1)}, u32[]{:S(2)}, u32[]{:S(2)}) %collective-permute-start.3) | collective-permute-done | bytes 524320 | tf_op jit(solution)/shard_map/ppermute | solution.py:22
  51.6 37.9 %reduce-scatter.3.cloned.1.call-done = f32[256,768]{0,1:T(8,128)} async-done(((f32[512,768]{0,1:T(8,128)}), f32[256,768]{0,1:T(8,128)}) %reduce-scatter.3.cloned.1.call-update) | async-done | bytes 786448 | tf_op jit(solution)/shard_map/reduce_scatter | solution.py:71
  94.8 6.7 %all_gather.6 = bf16[512,256]{0,1:T(8,128)(2,1)S(1)} all-gather(bf16[256,256]{0,1:T(8,128)(2,1)S(1)} %pad_maximum_fusion.2), channel_id=1, replica_groups=mesh['ctx'=32,'tr'=2,'tc'=4] {'tr'}, dimensions={0}, use_global_device_ids=true | all-gather | bytes 393216 | tf_op jit(solution)/shard_map/all_gather | solution.py:150
  107.4 334.9 %while.22 = (s32[]{:T(128)}, bf16[512,256]{1,0:T(8,128)(2,1)}, f32[1,4,256]{2,1,0:T(4,128)S(1)}, f32[1,4,256]{2,1,0:T(4,128)S(1)}, f32[1,4,256,128]{3,2,1,0:T(8,...) while((s32[]{:T(128)}, bf16[512,256]{1,0:T(8,128)(2,1)}, ...), condition=%wide.region_18.19_spmd.clone, body=%wide.region_11.18_spmd.clone.sunk | while | flops 276142272 | bytes 10047672 | solution.py:158
  128.4 8.7 %collective-permute-start = (bf16[512,256]{1,0:T(8,128)(2,1)}, bf16[512,256]{1,0:T(8,128)(2,1)S(1)}, u32[]{:S(2)}, u32[]{:S(2)}) collective-permute-start(bf16[512,256]{1,0:T(8,128)(2,1)} %get-tuple-element.709), channel_id=1, source_target_pairs={{0,8},{8,16},{16,24},{24,32},{32,40},{40,48},{48,56},{56,64},{64,7... | collective-permute-start | bytes 786440 | tf_op jit(solution)/shard_map/while/body/eval_jaxpr/ppermute | solution.py:37
  150.0 6.0 %collective-permute-start = (bf16[512,256]{1,0:T(8,128)(2,1)}, bf16[512,256]{1,0:T(8,128)(2,1)S(1)}, u32[]{:S(2)}, u32[]{:S(2)}) collective-permute-start(bf16[512,256]{1,0:T(8,128)(2,1)} %get-tuple-element.709), channel_id=1, source_target_pairs={{0,8},{8,16},{16,24},{24,32},{32,40},{40,48},{48,56},{56,64},{64,7... | collective-permute-start | bytes 786440 | tf_op jit(solution)/shard_map/while/body/eval_jaxpr/ppermute | solution.py:37
  160.4 5.2 collective-permute-start
  169.9 9.6 %collective-permute-start = (bf16[512,256]{1,0:T(8,128)(2,1)}, bf16[512,256]{1,0:T(8,128)(2,1)S(1)}, u32[]{:S(2)}, u32[]{:S(2)}) collective-permute-start(bf16[512,256]{1,0:T(8,128)(2,1)} %get-tuple-element.709), channel_id=1, source_target_pairs={{0,8},{8,16},{16,24},{24,32},{32,40},{40,48},{48,56},{56,64},{64,7... | collective-permute-start | bytes 786440 | tf_op jit(solution)/shard_map/while/body/eval_jaxpr/ppermute | solution.py:37
  183.8 5.2 collective-permute-start
  193.3 5.2 collective-permute-start
  202.8 5.2 collective-permute-start
  250.3 8.5 %collective-permute-start = (bf16[512,256]{1,0:T(8,128)(2,1)}, bf16[512,256]{1,0:T(8,128)(2,1)S(1)}, u32[]{:S(2)}, u32[]{:S(2)}) collective-permute-start(bf16[512,256]{1,0:T(8,128)(2,1)} %get-tuple-element.709), channel_id=1, source_target_pairs={{0,8},{8,16},{16,24},{24,32},{32,40},{40,48},{48,56},{56,64},{64,7... | collective-permute-start | bytes 786440 | tf_op jit(solution)/shard_map/while/body/eval_jaxpr/ppermute | solution.py:37
  329.6 8.5 %collective-permute-start = (bf16[512,256]{1,0:T(8,128)(2,1)}, bf16[512,256]{1,0:T(8,128)(2,1)S(1)}, u32[]{:S(2)}, u32[]{:S(2)}) collective-permute-start(bf16[512,256]{1,0:T(8,128)(2,1)} %get-tuple-element.709), channel_id=1, source_target_pairs={{0,8},{8,16},{16,24},{24,32},{32,40},{40,48},{48,56},{56,64},{64,7... | collective-permute-start | bytes 786440 | tf_op jit(solution)/shard_map/while/body/eval_jaxpr/ppermute | solution.py:37
  351.9 8.5 %collective-permute-start = (bf16[512,256]{1,0:T(8,128)(2,1)}, bf16[512,256]{1,0:T(8,128)(2,1)S(1)}, u32[]{:S(2)}, u32[]{:S(2)}) collective-permute-start(bf16[512,256]{1,0:T(8,128)(2,1)} %get-tuple-element.709), channel_id=1, source_target_pairs={{0,8},{8,16},{16,24},{24,32},{32,40},{40,48},{48,56},{56,64},{64,7... | collective-permute-start | bytes 786440 | tf_op jit(solution)/shard_map/while/body/eval_jaxpr/ppermute | solution.py:37
  364.8 6.4 %collective-permute-start = (bf16[512,256]{1,0:T(8,128)(2,1)}, bf16[512,256]{1,0:T(8,128)(2,1)S(1)}, u32[]{:S(2)}, u32[]{:S(2)}) collective-permute-start(bf16[512,256]{1,0:T(8,128)(2,1)} %get-tuple-element.709), channel_id=1, source_target_pairs={{0,8},{8,16},{16,24},{24,32},{32,40},{40,48},{48,56},{56,64},{64,7... | collective-permute-start | bytes 786440 | tf_op jit(solution)/shard_map/while/body/eval_jaxpr/ppermute | solution.py:37
  375.5 10.8 %collective-permute-start = (bf16[512,256]{1,0:T(8,128)(2,1)}, bf16[512,256]{1,0:T(8,128)(2,1)S(1)}, u32[]{:S(2)}, u32[]{:S(2)}) collective-permute-start(bf16[512,256]{1,0:T(8,128)(2,1)} %get-tuple-element.709), channel_id=1, source_target_pairs={{0,8},{8,16},{16,24},{24,32},{32,40},{40,48},{48,56},{56,64},{64,7... | collective-permute-start | bytes 786440 | tf_op jit(solution)/shard_map/while/body/eval_jaxpr/ppermute | solution.py:37
  390.6 6.4 %collective-permute-start = (bf16[512,256]{1,0:T(8,128)(2,1)}, bf16[512,256]{1,0:T(8,128)(2,1)S(1)}, u32[]{:S(2)}, u32[]{:S(2)}) collective-permute-start(bf16[512,256]{1,0:T(8,128)(2,1)} %get-tuple-element.709), channel_id=1, source_target_pairs={{0,8},{8,16},{16,24},{24,32},{32,40},{40,48},{48,56},{56,64},{64,7... | collective-permute-start | bytes 786440 | tf_op jit(solution)/shard_map/while/body/eval_jaxpr/ppermute | solution.py:37
  401.3 10.8 %collective-permute-start = (bf16[512,256]{1,0:T(8,128)(2,1)}, bf16[512,256]{1,0:T(8,128)(2,1)S(1)}, u32[]{:S(2)}, u32[]{:S(2)}) collective-permute-start(bf16[512,256]{1,0:T(8,128)(2,1)} %get-tuple-element.709), channel_id=1, source_target_pairs={{0,8},{8,16},{16,24},{24,32},{32,40},{40,48},{48,56},{56,64},{64,7... | collective-permute-start | bytes 786440 | tf_op jit(solution)/shard_map/while/body/eval_jaxpr/ppermute | solution.py:37
  416.4 6.4 %collective-permute-start = (bf16[512,256]{1,0:T(8,128)(2,1)}, bf16[512,256]{1,0:T(8,128)(2,1)S(1)}, u32[]{:S(2)}, u32[]{:S(2)}) collective-permute-start(bf16[512,256]{1,0:T(8,128)(2,1)} %get-tuple-element.709), channel_id=1, source_target_pairs={{0,8},{8,16},{16,24},{24,32},{32,40},{40,48},{48,56},{56,64},{64,7... | collective-permute-start | bytes 786440 | tf_op jit(solution)/shard_map/while/body/eval_jaxpr/ppermute | solution.py:37
  427.1 10.8 %collective-permute-start = (bf16[512,256]{1,0:T(8,128)(2,1)}, bf16[512,256]{1,0:T(8,128)(2,1)S(1)}, u32[]{:S(2)}, u32[]{:S(2)}) collective-permute-start(bf16[512,256]{1,0:T(8,128)(2,1)} %get-tuple-element.709), channel_id=1, source_target_pairs={{0,8},{8,16},{16,24},{24,32},{32,40},{40,48},{48,56},{56,64},{64,7... | collective-permute-start | bytes 786440 | tf_op jit(solution)/shard_map/while/body/eval_jaxpr/ppermute | solution.py:37
  443.6 7.4 %all_gather.7 = bf16[512,512]{0,1:T(8,128)(2,1)S(1)} all-gather(bf16[256,512]{0,1:T(8,128)(2,1)S(1)} %bitcast.110), channel_id=1, replica_groups=mesh['ctx'=32,'tr'=2,'tc'=4] {'tr'}, dimensions={0}, use_global_device_ids=true | all-gather | bytes 786432 | tf_op jit(solution)/shard_map/all_gather | solution.py:165
  453.6 117.5 %reduce-scatter.5.cloned.1.call-done = bf16[128,2048]{1,0:T(8,128)(2,1)} async-done(((bf16[512,2048]{1,0:T(8,128)(2,1)}), bf16[128,2048]{1,0:T(8,128)(2,1)}) %reduce-scatter.5.cloned.1.call-update) | async-done | bytes 524304 | tf_op jit(solution)/shard_map/reduce_scatter | solution.py:169
  (223 shorter events, 260.5 us)
Async XLA Ops:
  6.5 83.0 %reduce-scatter.3.cloned.1.call-start = ((), (), s32[]{:S(2)}) async-start(), calls=%async_computation.2 | async-start | bytes 2359296 | tf_op jit(solution)/shard_map/reduce_scatter | solution.py:71
  16.8 11.2 %collective-permute-start.1 = (bf16[128,2048]{1,0:T(8,128)(2,1)}, bf16[128,2048]{1,0:T(8,128)(2,1)S(1)}, u32[]{:S(2)}, u32[]{:S(2)}) collective-permute-start(bf16[128,2048]{1,0:T(8,128)(2,1)} %get-tuple-element.603), channel_id=1, source_target_pairs={{0,1},{1,2},{2,3},{3,0},{4,5},{5,6},{6,7},{7,4},{8,9},{9,10},{10,1... | collective-permute-start | bytes 1572872 | tf_op jit(solution)/shard_map/ppermute | solution.py:22
  18.1 12.5 %collective-permute-start.2 = (bf16[128,2048]{1,0:T(8,128)(2,1)}, bf16[128,2048]{1,0:T(8,128)(2,1)}, u32[]{:S(2)}, u32[]{:S(2)}) collective-permute-start(bf16[128,2048]{1,0:T(8,128)(2,1)} %get-tuple-element.603), channel_id=1, source_target_pairs={{0,3},{1,0},{2,1},{3,2},{4,7},{5,4},{6,5},{7,6},{8,11},{9,8},{10,9... | collective-permute-start | bytes 1572872 | tf_op jit(solution)/shard_map/ppermute | solution.py:27
  28.0 11.4 %collective-permute-start.3 = (bf16[128,2048]{1,0:T(8,128)(2,1)S(1)}, bf16[128,2048]{1,0:T(8,128)(2,1)}, u32[]{:S(2)}, u32[]{:S(2)}) collective-permute-start(bf16[128,2048]{1,0:T(8,128)(2,1)S(1)} %collective-permute-done.1), channel_id=1, source_target_pairs={{0,1},{1,2},{2,3},{3,0},{4,5},{5,6},{6,7},{7,4},{8,9},{9,10},{10,1... | collective-permute-start | bytes 1572872 | tf_op jit(solution)/shard_map/ppermute | solution.py:22
  50.5 520.6 %reduce-scatter.5.cloned.1.call-start = ((), (), s32[]{:S(2)}) async-start(), calls=%async_computation.3 | async-start | bytes 2621440 | tf_op jit(solution)/shard_map/reduce_scatter | solution.py:169
  128.4 12.3 %collective-permute-start = (bf16[512,256]{1,0:T(8,128)(2,1)}, bf16[512,256]{1,0:T(8,128)(2,1)S(1)}, u32[]{:S(2)}, u32[]{:S(2)}) collective-permute-start(bf16[512,256]{1,0:T(8,128)(2,1)} %get-tuple-element.709), channel_id=1, source_target_pairs={{0,8},{8,16},{16,24},{24,32},{32,40},{40,48},{48,56},{56,64},{64,7... | collective-permute-start | bytes 786440 | tf_op jit(solution)/shard_map/while/body/eval_jaxpr/ppermute | solution.py:37
  150.0 9.6 %collective-permute-start = (bf16[512,256]{1,0:T(8,128)(2,1)}, bf16[512,256]{1,0:T(8,128)(2,1)S(1)}, u32[]{:S(2)}, u32[]{:S(2)}) collective-permute-start(bf16[512,256]{1,0:T(8,128)(2,1)} %get-tuple-element.709), channel_id=1, source_target_pairs={{0,8},{8,16},{16,24},{24,32},{32,40},{40,48},{48,56},{56,64},{64,7... | collective-permute-start | bytes 786440 | tf_op jit(solution)/shard_map/while/body/eval_jaxpr/ppermute | solution.py:37
  160.4 8.8 %collective-permute-start = (bf16[512,256]{1,0:T(8,128)(2,1)}, bf16[512,256]{1,0:T(8,128)(2,1)S(1)}, u32[]{:S(2)}, u32[]{:S(2)}) collective-permute-start(bf16[512,256]{1,0:T(8,128)(2,1)} %get-tuple-element.709), channel_id=1, source_target_pairs={{0,8},{8,16},{16,24},{24,32},{32,40},{40,48},{48,56},{56,64},{64,7... | collective-permute-start | bytes 786440 | tf_op jit(solution)/shard_map/while/body/eval_jaxpr/ppermute | solution.py:37
  169.9 13.2 %collective-permute-start = (bf16[512,256]{1,0:T(8,128)(2,1)}, bf16[512,256]{1,0:T(8,128)(2,1)S(1)}, u32[]{:S(2)}, u32[]{:S(2)}) collective-permute-start(bf16[512,256]{1,0:T(8,128)(2,1)} %get-tuple-element.709), channel_id=1, source_target_pairs={{0,8},{8,16},{16,24},{24,32},{32,40},{40,48},{48,56},{56,64},{64,7... | collective-permute-start | bytes 786440 | tf_op jit(solution)/shard_map/while/body/eval_jaxpr/ppermute | solution.py:37
  183.8 8.8 %collective-permute-start = (bf16[512,256]{1,0:T(8,128)(2,1)}, bf16[512,256]{1,0:T(8,128)(2,1)S(1)}, u32[]{:S(2)}, u32[]{:S(2)}) collective-permute-start(bf16[512,256]{1,0:T(8,128)(2,1)} %get-tuple-element.709), channel_id=1, source_target_pairs={{0,8},{8,16},{16,24},{24,32},{32,40},{40,48},{48,56},{56,64},{64,7... | collective-permute-start | bytes 786440 | tf_op jit(solution)/shard_map/while/body/eval_jaxpr/ppermute | solution.py:37
  193.3 8.8 %collective-permute-start = (bf16[512,256]{1,0:T(8,128)(2,1)}, bf16[512,256]{1,0:T(8,128)(2,1)S(1)}, u32[]{:S(2)}, u32[]{:S(2)}) collective-permute-start(bf16[512,256]{1,0:T(8,128)(2,1)} %get-tuple-element.709), channel_id=1, source_target_pairs={{0,8},{8,16},{16,24},{24,32},{32,40},{40,48},{48,56},{56,64},{64,7... | collective-permute-start | bytes 786440 | tf_op jit(solution)/shard_map/while/body/eval_jaxpr/ppermute | solution.py:37
  202.8 8.8 %collective-permute-start = (bf16[512,256]{1,0:T(8,128)(2,1)}, bf16[512,256]{1,0:T(8,128)(2,1)S(1)}, u32[]{:S(2)}, u32[]{:S(2)}) collective-permute-start(bf16[512,256]{1,0:T(8,128)(2,1)} %get-tuple-element.709), channel_id=1, source_target_pairs={{0,8},{8,16},{16,24},{24,32},{32,40},{40,48},{48,56},{56,64},{64,7... | collective-permute-start | bytes 786440 | tf_op jit(solution)/shard_map/while/body/eval_jaxpr/ppermute | solution.py:37
  212.3 8.8 %collective-permute-start = (bf16[512,256]{1,0:T(8,128)(2,1)}, bf16[512,256]{1,0:T(8,128)(2,1)S(1)}, u32[]{:S(2)}, u32[]{:S(2)}) collective-permute-start(bf16[512,256]{1,0:T(8,128)(2,1)} %get-tuple-element.709), channel_id=1, source_target_pairs={{0,8},{8,16},{16,24},{24,32},{32,40},{40,48},{48,56},{56,64},{64,7... | collective-permute-start | bytes 786440 | tf_op jit(solution)/shard_map/while/body/eval_jaxpr/ppermute | solution.py:37
  221.8 8.8 %collective-permute-start = (bf16[512,256]{1,0:T(8,128)(2,1)}, bf16[512,256]{1,0:T(8,128)(2,1)S(1)}, u32[]{:S(2)}, u32[]{:S(2)}) collective-permute-start(bf16[512,256]{1,0:T(8,128)(2,1)} %get-tuple-element.709), channel_id=1, source_target_pairs={{0,8},{8,16},{16,24},{24,32},{32,40},{40,48},{48,56},{56,64},{64,7... | collective-permute-start | bytes 786440 | tf_op jit(solution)/shard_map/while/body/eval_jaxpr/ppermute | solution.py:37
  250.3 12.1 %collective-permute-start = (bf16[512,256]{1,0:T(8,128)(2,1)}, bf16[512,256]{1,0:T(8,128)(2,1)S(1)}, u32[]{:S(2)}, u32[]{:S(2)}) collective-permute-start(bf16[512,256]{1,0:T(8,128)(2,1)} %get-tuple-element.709), channel_id=1, source_target_pairs={{0,8},{8,16},{16,24},{24,32},{32,40},{40,48},{48,56},{56,64},{64,7... | collective-permute-start | bytes 786440 | tf_op jit(solution)/shard_map/while/body/eval_jaxpr/ppermute | solution.py:37
  263.1 8.8 %collective-permute-start = (bf16[512,256]{1,0:T(8,128)(2,1)}, bf16[512,256]{1,0:T(8,128)(2,1)S(1)}, u32[]{:S(2)}, u32[]{:S(2)}) collective-permute-start(bf16[512,256]{1,0:T(8,128)(2,1)} %get-tuple-element.709), channel_id=1, source_target_pairs={{0,8},{8,16},{16,24},{24,32},{32,40},{40,48},{48,56},{56,64},{64,7... | collective-permute-start | bytes 786440 | tf_op jit(solution)/shard_map/while/body/eval_jaxpr/ppermute | solution.py:37
  329.6 12.1 %collective-permute-start = (bf16[512,256]{1,0:T(8,128)(2,1)}, bf16[512,256]{1,0:T(8,128)(2,1)S(1)}, u32[]{:S(2)}, u32[]{:S(2)}) collective-permute-start(bf16[512,256]{1,0:T(8,128)(2,1)} %get-tuple-element.709), channel_id=1, source_target_pairs={{0,8},{8,16},{16,24},{24,32},{32,40},{40,48},{48,56},{56,64},{64,7... | collective-permute-start | bytes 786440 | tf_op jit(solution)/shard_map/while/body/eval_jaxpr/ppermute | solution.py:37
  351.9 12.2 %collective-permute-start = (bf16[512,256]{1,0:T(8,128)(2,1)}, bf16[512,256]{1,0:T(8,128)(2,1)S(1)}, u32[]{:S(2)}, u32[]{:S(2)}) collective-permute-start(bf16[512,256]{1,0:T(8,128)(2,1)} %get-tuple-element.709), channel_id=1, source_target_pairs={{0,8},{8,16},{16,24},{24,32},{32,40},{40,48},{48,56},{56,64},{64,7... | collective-permute-start | bytes 786440 | tf_op jit(solution)/shard_map/while/body/eval_jaxpr/ppermute | solution.py:37
  364.8 10.0 %collective-permute-start = (bf16[512,256]{1,0:T(8,128)(2,1)}, bf16[512,256]{1,0:T(8,128)(2,1)S(1)}, u32[]{:S(2)}, u32[]{:S(2)}) collective-permute-start(bf16[512,256]{1,0:T(8,128)(2,1)} %get-tuple-element.709), channel_id=1, source_target_pairs={{0,8},{8,16},{16,24},{24,32},{32,40},{40,48},{48,56},{56,64},{64,7... | collective-permute-start | bytes 786440 | tf_op jit(solution)/shard_map/while/body/eval_jaxpr/ppermute | solution.py:37
  375.5 14.4 %collective-permute-start = (bf16[512,256]{1,0:T(8,128)(2,1)}, bf16[512,256]{1,0:T(8,128)(2,1)S(1)}, u32[]{:S(2)}, u32[]{:S(2)}) collective-permute-start(bf16[512,256]{1,0:T(8,128)(2,1)} %get-tuple-element.709), channel_id=1, source_target_pairs={{0,8},{8,16},{16,24},{24,32},{32,40},{40,48},{48,56},{56,64},{64,7... | collective-permute-start | bytes 786440 | tf_op jit(solution)/shard_map/while/body/eval_jaxpr/ppermute | solution.py:37
  390.6 10.0 %collective-permute-start = (bf16[512,256]{1,0:T(8,128)(2,1)}, bf16[512,256]{1,0:T(8,128)(2,1)S(1)}, u32[]{:S(2)}, u32[]{:S(2)}) collective-permute-start(bf16[512,256]{1,0:T(8,128)(2,1)} %get-tuple-element.709), channel_id=1, source_target_pairs={{0,8},{8,16},{16,24},{24,32},{32,40},{40,48},{48,56},{56,64},{64,7... | collective-permute-start | bytes 786440 | tf_op jit(solution)/shard_map/while/body/eval_jaxpr/ppermute | solution.py:37
  401.3 14.4 %collective-permute-start = (bf16[512,256]{1,0:T(8,128)(2,1)}, bf16[512,256]{1,0:T(8,128)(2,1)S(1)}, u32[]{:S(2)}, u32[]{:S(2)}) collective-permute-start(bf16[512,256]{1,0:T(8,128)(2,1)} %get-tuple-element.709), channel_id=1, source_target_pairs={{0,8},{8,16},{16,24},{24,32},{32,40},{40,48},{48,56},{56,64},{64,7... | collective-permute-start | bytes 786440 | tf_op jit(solution)/shard_map/while/body/eval_jaxpr/ppermute | solution.py:37
  416.4 10.0 %collective-permute-start = (bf16[512,256]{1,0:T(8,128)(2,1)}, bf16[512,256]{1,0:T(8,128)(2,1)S(1)}, u32[]{:S(2)}, u32[]{:S(2)}) collective-permute-start(bf16[512,256]{1,0:T(8,128)(2,1)} %get-tuple-element.709), channel_id=1, source_target_pairs={{0,8},{8,16},{16,24},{24,32},{32,40},{40,48},{48,56},{56,64},{64,7... | collective-permute-start | bytes 786440 | tf_op jit(solution)/shard_map/while/body/eval_jaxpr/ppermute | solution.py:37
  427.1 14.4 %collective-permute-start = (bf16[512,256]{1,0:T(8,128)(2,1)}, bf16[512,256]{1,0:T(8,128)(2,1)S(1)}, u32[]{:S(2)}, u32[]{:S(2)}) collective-permute-start(bf16[512,256]{1,0:T(8,128)(2,1)} %get-tuple-element.709), channel_id=1, source_target_pairs={{0,8},{8,16},{16,24},{24,32},{32,40},{40,48},{48,56},{56,64},{64,7... | collective-permute-start | bytes 786440 | tf_op jit(solution)/shard_map/while/body/eval_jaxpr/ppermute | solution.py:37
  (19 other events, 583.1 us)
Sparse Core Ops, SparseCore 0:
  50.7 38.8 reduce-scatter.2
  453.8 117.3 reduce-scatter.4
